TPU v7x, 128 devices: a whole 4x4x4 slice. The times are simulated.
128 devices in a mesh: pb: 8 (over z, x_lo), dev: 16 (over y, x_hi, core).
Axes of the slice: x: 4 (x_hi: 2, x_lo: 2; x = x_hi * 2 + x_lo), y: 4, z: 4, core: 2. Of those that a mesh axis runs over, the one named last changes fastest.
Arguments:
- q_hidden: bfloat16 [16384, 1024], P(('pb', 'dev')), may hold values from -60 to 60
- d_hidden: bfloat16 [16384, 1024], P(('dev', 'pb')), may hold values from -60 to 60
- positive: int32 [16384], P(('pb', 'dev')), may hold values from 0 to 16383, each once
- query_part: int32 [16384], P(('pb', 'dev')), may hold values from 0 to 7
- doc_part: int32 [16384], P(('dev', 'pb')), may hold values from 0 to 7
- loss_weight: bfloat16 [16384], P(('pb', 'dev')), may hold values from 0.5 to 5
- norm_gain: float32 [1024], replicated, may hold values from 0.5 to 1.5
- norm_bias: float32 [1024], replicated, may hold values from -1.8 to 1.8
- proj: bfloat16 [1024, 1024], replicated, may hold values from -0.1875 to 0.1875
Outputs:
- dq_hidden: bfloat16 [16384, 1024], P(('pb', 'dev'))
- dd_hidden: bfloat16 [16384, 1024], P(('dev', 'pb'))
- d_proj: float32 [1024, 1024], P('pb', 'dev')
- d_gain: float32 [1024], replicated
- d_bias: float32 [1024], replicated
Inputs may be any that keep to these rules, and one draw needn't show every extreme that they name: `positive`: each document index names the clicked document of exactly one query.
All inputs are finite; a program needn't handle non-finite values.
Results may differ from a plain program's by a relative error of at most 0.024.
Values may be sent and summed in bfloat16 or wider, within the bound.
A program may use at most 128 MiB of HBM per device.

v0:
```python
import jax
import jax.numpy as jnp
from jax import lax
from jax.experimental import pallas as pl
from jax.experimental.pallas import tpu as pltpu
from jax.sharding import PartitionSpec as P

logit_scale = 100.0
f32, bf16 = jnp.float32, jnp.bfloat16
MESH = pl.DeviceIdType.MESH
rows, width = 128, 1024
half = rows // 2
copies = 160
OFFSETS = ((0, 0), (1, 0), (0, 1), (0, 3), (0, 2), (1, 2), (1, 1), (1, 3))
NT = (((1,), (1,)), ((), ()))


def kernel(
    qh_hbm, dh_hbm, pos_hbm, qpart_hbm, weight_hbm, dpart_hbm, gain_hbm, bias_hbm, proj_hbm,
    dq, dd, dproj, dgain, dbias,
    qh, dh, pos_in, qpart_in, weight_in, dpart_in, gain, bias,
    proj, qbuf, dbuf, dt, st, gt, unit, normed, recip, inv, out_t, lab_q, lab_d, labs, dlab, dcol, mst, sst, lsend, lbuf,
    lsef, lrel, gqp, cbuf, sbuf, qfold, qring, qx, gdp, dfold, dring, dx_buf,
    ge, hp, hc, hs, hz1, hy1, h0, h1, hy2, hz2, hx, hx3, gb, gba, gbb,
    send_sem, recv_sem, local_sem,
):
    pb, dev = lax.axis_index("pb"), lax.axis_index("dev")
    z, xl = pb // 2, lax.rem(pb, 2)
    y, xh, core = dev // 4, lax.rem(dev // 2, 2), lax.rem(dev, 2)

    def q_peer(dx, dy, dc=0):
        return (z * 2 + lax.rem(xl + dx, 2), lax.rem(y + dy, 4) * 4 + xh * 2 + lax.rem(core + dc, 2))

    def d_peer(dx, dz):
        return (lax.rem(z + dz, 4) * 2 + lax.rem(xl + dx, 2), y * 4 + lax.rem(xh + dx, 2) * 2 + core)

    def x_peer(dh, dl):
        return (z * 2 + lax.rem(xl + dl, 2), y * 4 + lax.rem(xh + dh, 2) * 2 + core)

    started = []

    def send(src, dst, peer):
        n = len(started)
        copy = pltpu.make_async_remote_copy(
            src_ref=src, dst_ref=dst, send_sem=send_sem.at[n], recv_sem=recv_sem.at[n],
            device_id=peer, device_id_type=MESH,
        )
        copy.start()
        started.append(copy)
        return copy

    def arrive(*copies):
        for copy in copies:
            copy.wait_recv()

    q_offsets = [(dx, dy, dc) for dx in range(2) for dy in range(4) for dc in range(2)]
    d_offsets = [(dx, dz) for dx in range(2) for dz in range(4)]

    loads = []
    for n, (src, dst) in enumerate((
        (qh_hbm, qh), (dh_hbm, dh), (proj_hbm, proj), (gain_hbm, gain), (bias_hbm, bias),
        (pos_hbm, pos_in), (qpart_hbm, qpart_in), (weight_hbm, weight_in), (dpart_hbm, dpart_in),
    )):
        loads.append(pltpu.make_async_copy(src, dst, local_sem.at[n]))
        loads[-1].start()
    barrier = pltpu.get_barrier_semaphore()
    peers = [q_peer(*o) for o in q_offsets[1:]] + [d_peer(*o) for o in d_offsets[1:]] + [x_peer(1, 0)]
    for peer in peers:
        pl.semaphore_signal(barrier, inc=1, device_id=peer, device_id_type=MESH)

    for n in (0, 1, 3, 4, 5, 6, 7, 8):
        loads[n].wait()
    lab_q[...] = jnp.zeros((8, rows), f32)
    lab_q[0:1, :] = pos_in[...].astype(f32)
    lab_q[1:2, :] = qpart_in[...].astype(f32)
    lab_q[2:3, :] = weight_in[...].astype(f32)
    lab_d[...] = jnp.broadcast_to(dpart_in[...].astype(f32), (8, rows))
    values = jnp.concatenate([qh[...], dh[...]], axis=0).astype(f32)
    centred = values - jnp.mean(values, axis=1, keepdims=True)
    r = lax.rsqrt(jnp.mean(centred * centred, axis=1, keepdims=True) + 1e-05)
    norm = centred * r
    recip[...] = r
    normed[...] = norm
    normal_out = (norm * gain[...] + bias[...]).astype(bf16)
    loads[2].wait()
    pl.semaphore_wait(barrier, len(peers))

    block = 8 * rows

    def q_at(core_index, k, offset=0):
        return pl.multiple_of(core_index * block + k * rows + offset, half)

    lab_copies = []
    for dx, dy, dc in q_offsets[1:]:
        k = OFFSETS.index((dx, (4 - dy) % 4))
        dst = labs.at[:, pl.ds(pl.multiple_of(core * block + k * rows, rows), rows)]
        lab_copies.append(send(lab_q, dst, q_peer(dx, dy, dc)))
    for dx, dz in d_offsets[1:]:
        lab_copies.append(send(lab_d, dlab.at[OFFSETS.index((dx, (4 - dz) % 4))], d_peer(dx, dz)))
    labs[:, pl.ds(pl.multiple_of(core * block, rows), rows)] = lab_q[...]
    dlab[0] = lab_d[...]

    embed = jnp.dot(normal_out, proj[...], preferred_element_type=f32)
    i = lax.rsqrt(jnp.sum(embed * embed, axis=1, keepdims=True) + 1e-06)
    inv[...] = i
    u = embed * i
    unit[...] = u
    qbuf[pl.ds(q_at(core, 0), rows), :] = u[:rows].astype(bf16)
    dbuf[0:rows, :] = u[rows:].astype(bf16)

    def q_half(k, h):
        return qbuf.at[pl.ds(q_at(core, k, h * half), half), :]

    def d_half(k, h):
        return dbuf.at[pl.ds(k * rows + h * half, half), :]

    def to_sibling(k):
        part = qbuf.at[pl.ds(pl.multiple_of(core * block + k * rows, rows), rows), :]
        return send(part, part, q_peer(0, 0, 1))

    q_got, d_got, sib = {}, {}, {}

    def hop(part, got, peer, k, h, to, way):
        got[to, h] = send(part(k, h), part(to, h), peer(1, 0) if way == 0 else peer(0, way))

    towers = ((q_half, q_got, q_peer), (d_half, d_got, d_peer))
    for h in range(2):
        for tower in towers:
            hop(*tower, 0, h, 3, 1)
            hop(*tower, 0, 1 - h, 2, 3)
            hop(*tower, 0, h, 1, 0)
    sib[0] = to_sibling(0)
    out_t[...] = normal_out.T
    for tower in towers:
        arrive(tower[1][3, 0])
        hop(*tower, 3, 0, 4, 1)
        arrive(tower[1][2, 1])
        hop(*tower, 2, 1, 4, 3)
    for tower in towers:
        arrive(tower[1][1, 0])
        hop(*tower, 1, 0, 7, 1)
    for tower in towers:
        arrive(tower[1][1, 1])
        hop(*tower, 1, 1, 6, 3)
        hop(*tower, 1, 1, 7, 1)
        hop(*tower, 1, 0, 6, 3)
    sib[1] = to_sibling(1)
    arrive(q_got[3, 1], q_got[2, 0])
    sib[2], sib[3] = to_sibling(2), to_sibling(3)
    arrive(*lab_copies)
    arrive(d_got[3, 1], d_got[2, 0])

    for k in range(8):
        dcol[k * rows : (k + 1) * rows, :] = jnp.broadcast_to(dlab[k, 0:1, :], (rows, rows)).T

    def transpose_docs(first, count):
        for k in range(first, first + count):
            dt[:, k * rows : (k + 1) * rows] = dbuf[k * rows : (k + 1) * rows, :].T

    lane = lax.broadcasted_iota(jnp.int32, (rows, 2 * rows), 0).astype(f32)

    def bases(k):
        to_pb, to_dev = d_peer(*OFFSETS[k])
        return ((to_dev * 8 + to_pb) * rows).astype(f32)

    def pair_cols(core_index, m):
        return pl.ds(pl.multiple_of(core_index * block + m * 2 * rows, 2 * rows), 2 * rows)

    def score(first, count, piece, cols):
        s = logit_scale * lax.dot_general(
            dbuf[first * rows : (first + count) * rows, :], qbuf[cols, :], NT, preferred_element_type=f32
        )
        pos, part = labs[0:1, cols], labs[1:2, cols]
        masked = []
        for n in range(count):
            k = first + n
            col = dcol[k * rows : (k + 1) * rows, :]
            valid = jnp.logical_or(part != jnp.concatenate([col, col], axis=1), lane == pos - bases(k))
            masked.append(jnp.where(valid, s[n * rows : (n + 1) * rows], jnp.float32(-1e30)))
        top = jnp.full((1, 2 * rows), -1e4, f32)
        for m in masked:
            top = jnp.maximum(top, jnp.max(m, axis=0, keepdims=True))
        total = jnp.zeros((1, 2 * rows), f32)
        for n, m in enumerate(masked):
            p = jnp.exp(m - top)
            total = total + jnp.sum(p, axis=0, keepdims=True)
            st[(first + n) * rows : (first + n + 1) * rows, cols] = p
        mst[piece, :, cols] = top
        sst[piece, :, cols] = total

    pieces = ((0, 4), (4, 2), (6, 2))

    def scores(piece, pairs):
        low, step, count = pairs

        def body(n, carry):
            m, c = low + step * (n // 2), lax.rem(n, 2)
            score(*pieces[piece], piece, pair_cols(c, m))
            return carry

        lax.fori_loop(0, 2 * count, body, 0)

    transpose_docs(0, 4)
    arrive(sib[0], sib[1], sib[2], sib[3])
    scores(0, (0, 1, 2))

    for tower in towers:
        arrive(tower[1][7, 0])
        hop(*tower, 7, 0, 5, 1)
        arrive(tower[1][6, 1])
        hop(*tower, 6, 1, 5, 3)
    arrive(q_got[7, 1], q_got[6, 0])
    sib[6], sib[7] = to_sibling(6), to_sibling(7)
    arrive(q_got[4, 0], q_got[4, 1])
    sib[4] = to_sibling(4)
    arrive(d_got[7, 1], d_got[6, 0], d_got[4, 0], d_got[4, 1])
    transpose_docs(6, 2)
    transpose_docs(4, 1)
    scores(2, (0, 1, 2))
    arrive(sib[6], sib[7])
    scores(0, (3, 1, 1))
    scores(2, (3, 1, 1))

    arrive(q_got[5, 0], q_got[5, 1])
    sib[5] = to_sibling(5)
    arrive(d_got[5, 0], d_got[5, 1])
    transpose_docs(5, 1)
    scores(1, (0, 1, 2))
    scores(1, (3, 1, 1))
    arrive(sib[4], sib[5])
    scores(0, (2, 1, 1))
    scores(1, (2, 1, 1))
    scores(2, (2, 1, 1))

    top = jnp.maximum(jnp.maximum(mst[0], mst[1]), mst[2])
    total = sum(sst[b] * jnp.exp(mst[b] - top) for b in range(3))
    local = top + jnp.log(jnp.maximum(total, 1e-37))
    places = []
    for n in range(16):
        c, (dx, dy) = n // 8, OFFSETS[n % 8]
        place = c * block + (lax.rem(y + dy, 4) * 2 + lax.rem(xl + dx, 2)) * rows
        places.append(pl.ds(pl.multiple_of(place, rows), rows))
        lsend[:, places[-1]] = local[:, n * rows : (n + 1) * rows]
    lse_copies = [send(lsend, lbuf.at[s], q_peer(*q_offsets[s])) for s in range(1, 16)]
    lbuf[0] = lsend[...]
    arrive(*lse_copies)
    every = [lbuf[s] for s in range(16)]
    top = every[0]
    for e in every[1:]:
        top = jnp.maximum(top, e)
    total = sum(jnp.exp(e - top) for e in every)
    lsef[...] = top + jnp.log(total)
    for n, place in enumerate(places):
        lrel[:, n * rows : (n + 1) * rows] = lsef[:, place]
    for b in range(3):
        sst[b] = jnp.exp(mst[b] - lrel[...])

    def grads(g, carry):
        cols = pl.ds(pl.multiple_of(g * 2 * rows, 2 * rows), 2 * rows)
        pos, weight = labs[0:1, cols], labs[2:3, cols]
        for k in range(8):
            scale = sst[0 if k < 4 else 1 if k < 6 else 2, :, cols]
            hit = jnp.where(lane == pos - bases(k), jnp.float32(1), jnp.float32(0))
            prob = st[k * rows : (k + 1) * rows, cols] * scale
            gt[k * rows : (k + 1) * rows, cols] = (weight * (prob - hit)).astype(bf16)
        return carry

    lax.fori_loop(0, 8, grads, 0)

    def doc_terms(m):
        def body(j, carry):
            cols = pl.ds(pl.multiple_of(j * 256, 256), 256)
            v = jnp.dot(
                gt[2 * m * rows : 2 * (m + 1) * rows, :], qbuf[:, cols], preferred_element_type=f32
            ).astype(bf16)
            gdp[2 * m, :, cols] = v[:rows]
            gdp[2 * m + 1, :, cols] = v[rows:]
            return carry

        lax.fori_loop(0, 4, body, 0)

    cores = {}

    def query_terms(m, other):
        cols = pair_cols(1 - core if other else core, m)

        def body(j, carry):
            part = pl.ds(pl.multiple_of(j * 512, 512), 512)
            v = jnp.dot(dt[part, :], gt[:, cols], preferred_element_type=f32).astype(bf16)
            gqp[other, 2 * m, part, :] = v[:, :rows]
            gqp[other, 2 * m + 1, part, :] = v[:, rows:]
            return carry

        lax.fori_loop(0, 2, body, 0)
        if other:
            span = pl.ds(2 * m, 2)
            cores[m] = send(gqp.at[1, span], cbuf.at[span], q_peer(0, 0, 1))

    def both_cores(k):
        if k // 2 in cores:
            arrive(cores.pop(k // 2))
        sbuf[k] = (gqp[0, k].astype(f32) + cbuf[k].astype(f32)).astype(bf16)

    slots = ((0, 2, 3, 4), (1, 6, 7, 5))

    def far_terms(src, fold, ring, peer, h, dx):
        far = slots[dx][3]
        return [
            send(src.at[far, pl.ds(0, h), :], fold.at[dx, 0], peer(0, 1)),
            send(src.at[far, pl.ds(h, h), :], fold.at[dx, 1], peer(0, 3)),
        ]

    def near_terms(src, fold, ring, peer, h, dx):
        _, plus, minus, _ = slots[dx]
        return [
            send(src.at[plus, pl.ds(h, h), :], ring.at[dx, 0, pl.ds(h, h), :], peer(0, 1)),
            send(src.at[minus, pl.ds(0, h), :], ring.at[dx, 1, pl.ds(0, h), :], peer(0, 3)),
        ]

    def merged(src, fold, ring, peer, h, dx, waits):
        _, plus, minus, _ = slots[dx]
        arrive(waits[0])
        src[plus, 0:h, :] = (src[plus, 0:h, :].astype(f32) + fold[dx, 0].astype(f32)).astype(bf16)
        a = send(src.at[plus, pl.ds(0, h), :], ring.at[dx, 0, pl.ds(0, h), :], peer(0, 1))
        arrive(waits[1])
        src[minus, h : 2 * h, :] = (src[minus, h : 2 * h, :].astype(f32) + fold[dx, 1].astype(f32)).astype(bf16)
        b = send(src.at[minus, pl.ds(h, h), :], ring.at[dx, 1, pl.ds(h, h), :], peer(0, 3))
        return [a, b]

    def ring_sum(src, ring, dx, waits):
        arrive(*waits)
        return src[dx].astype(f32) + ring[dx, 0].astype(f32) + ring[dx, 1].astype(f32)

    D = (gdp, dfold, dring, d_peer, half)
    Q = (sbuf, qfold, qring, q_peer, width // 2)
    query_terms(2, 1)
    query_terms(2, 0)
    query_terms(3, 1)
    doc_terms(2)
    d_fold1 = far_terms(*D, 1)
    both_cores(5)
    q_fold1 = far_terms(*Q, 1)
    query_terms(3, 0)
    both_cores(6)
    both_cores(7)
    q_ring1 = near_terms(*Q, 1)
    doc_terms(3)
    d_ring1 = near_terms(*D, 1)
    both_cores(4)
    query_terms(1, 1)
    query_terms(0, 1)
    query_terms(1, 0)
    d_ring1 += merged(*D, 1, d_fold1)
    d_fold0 = far_terms(*D, 0)
    q_ring1 += merged(*Q, 1, q_fold1)
    q_fold0 = far_terms(*Q, 0)
    doc_terms(1)
    d_ring0 = near_terms(*D, 0)
    both_cores(2)
    both_cores(3)
    q_ring0 = near_terms(*Q, 0)
    query_terms(0, 0)
    doc_terms(0)
    both_cores(1)
    both_cores(0)
    dx_buf[0] = ring_sum(gdp, dring, 1, d_ring1).astype(bf16)
    d_across = send(dx_buf.at[0], dx_buf.at[1], d_peer(1, 0))
    qx[0] = ring_sum(sbuf, qring, 1, q_ring1).astype(bf16)
    q_across = send(qx.at[0], qx.at[1], q_peer(1, 0))
    d_ring0 += merged(*D, 0, d_fold0)
    q_ring0 += merged(*Q, 0, q_fold0)

    def backward(g_unit, low, out):
        span = slice(low, low + rows)
        uu, nn = unit[span, :], normed[span, :]
        g = ((g_unit - uu * jnp.sum(uu * g_unit, axis=1, keepdims=True)) * inv[span, :]).astype(bf16)
        ge[span, :] = g
        gn = lax.dot_general(g, proj[...], NT, preferred_element_type=f32)
        scaled = gn * gain[...]
        out[...] = (
            recip[span, :]
            * (scaled - jnp.mean(scaled, axis=1, keepdims=True) - nn * jnp.mean(scaled * nn, axis=1, keepdims=True))
        ).astype(bf16)
        return jnp.sum(gn * nn, axis=0, keepdims=True), jnp.sum(gn, axis=0, keepdims=True)

    g_doc = ring_sum(gdp, dring, 0, d_ring0)
    arrive(d_across)
    g_doc = logit_scale * (g_doc + dx_buf[1].astype(f32))
    g_query = ring_sum(sbuf, qring, 0, q_ring0)
    arrive(q_across)
    gain_d, bias_d = backward(g_doc, rows, dd)
    gain_q, bias_q = backward(logit_scale * (g_query + qx[1].astype(f32)).T, 0, dq)

    gb[0:1, :] = gain_d + gain_q
    gb[1:2, :] = bias_d + bias_q
    order = (y * 2 + xl) * 2 + core
    gb_copies = [send(gb, gba.at[order], q_peer(*o)) for o in q_offsets[1:]]
    gba[order] = gb[...]

    left = lax.broadcasted_iota(jnp.int32, (half, rows), 1) < half

    def head(n, carry):
        for a in range(2):
            v = jnp.dot(
                out_t[pl.ds(pl.multiple_of((2 * n + a) * rows, rows), rows), :], ge[...], preferred_element_type=f32
            )
            for j in range(8):
                upper, lower = v[:half, j * rows : (j + 1) * rows], v[half:, j * rows : (j + 1) * rows]
                hp[0, a, j % 2, j // 2, n] = jnp.where(left, upper, pltpu.roll(lower, half, 1)).astype(bf16)
                hp[1, a, j % 2, j // 2, n] = jnp.where(left, pltpu.roll(upper, half, 1), lower).astype(bf16)
        return carry

    lax.fori_loop(0, 4, head, 0)
    head_core = [send(hp.at[1 - core, a], hc.at[a], q_peer(0, 0, 1)) for a in range(2)]
    first = []
    for a in range(2):
        arrive(head_core[a])

        def add_cores(n, carry):
            for b in range(2):
                hs[a, b, n] = (hp[core, a, b, n].astype(f32) + hc[a, b, n].astype(f32)).astype(bf16)
            return carry

        lax.fori_loop(0, 4, add_cores, 0)
        for s in range(1, 4):
            zz, yy = lax.rem(z + s, 4), lax.rem(y + s, 4)
            if a == 0:
                first.append(send(hs.at[0, :, :, zz], hz1.at[s - 1], d_peer(0, s)))
            else:
                first.append(send(hs.at[1, :, yy], hy1.at[s - 1], q_peer(0, s)))

    arrive(*gb_copies)
    acc = gba[0]
    for n in range(1, 16):
        acc = acc + gba[n]
    order = z * 2 + xh
    gbb[order] = acc
    gb_copies = [send(gbb.at[order], gbb.at[order], d_peer(*o)) for o in d_offsets[1:]]

    def total_of(own, got):
        return own.astype(f32) + sum(got[n].astype(f32) for n in range(3))

    arrive(*first[:3])
    h0[...] = total_of(hs[0, :, :, z], hz1).astype(bf16)
    second = [send(h0.at[:, lax.rem(y + s, 4)], hy2.at[s - 1], q_peer(0, s)) for s in range(1, 4)]
    arrive(*first[3:])
    h1[...] = total_of(hs[1, :, y], hy1).astype(bf16)
    second += [send(h1.at[:, lax.rem(z + s, 4)], hz2.at[s - 1], d_peer(0, s)) for s in range(1, 4)]
    arrive(*second)
    hx[0] = total_of(h0[:, y], hy2).astype(bf16)
    hx[1] = total_of(h1[:, z], hz2).astype(bf16)
    third = []
    for s, (sh, sl) in enumerate(((0, 1), (1, 0), (1, 1))):
        src = hx.at[lax.rem(xl + sl, 2), lax.rem(xh + sh, 2)]
        third.append(send(src, hx3.at[s], x_peer(sh, sl)))
    arrive(*third)
    final = total_of(hx[xl, xh], hx3)
    dproj[:, 0:half] = final[:, :half].T
    dproj[:, half:rows] = final[:, half:].T

    arrive(*gb_copies)
    acc = gbb[0]
    for n in range(1, 8):
        acc = acc + gbb[n]
    dgain[...] = acc[0:1]
    dbias[...] = acc[1:2]

    for copy in started:
        copy.wait_send()


def hand_over(*refs):
    for src, dst in zip(refs[:5], refs[5:]):
        dst[...] = src[...]


def per_device(
    q_hidden, d_hidden, positive, query_part, doc_part, loss_weight, norm_gain, norm_bias, proj
):
    vmem = pl.BlockSpec(memory_space=pltpu.VMEM)
    V = pltpu.VMEM
    e = width
    scratch = [
        V((rows, e), bf16),
        V((rows, e), bf16),
        V((1, rows), jnp.int32),
        V((1, rows), jnp.int32),
        V((1, rows), bf16),
        V((1, rows), jnp.int32),
        V((1, e), f32),
        V((1, e), f32),
        V((e, e), bf16),
        V((16 * rows, e), bf16),
        V((8 * rows, e), bf16),
        V((e, 8 * rows), bf16),
        V((8 * rows, 16 * rows), f32),
        V((8 * rows, 16 * rows), bf16),
        V((2 * rows, e), f32),
        V((2 * rows, e), f32),
        V((2 * rows, 1), f32),
        V((2 * rows, 1), f32),
        V((e, 2 * rows), bf16),
        V((8, rows), f32),
        V((8, rows), f32),
        V((8, 16 * rows), f32),
        V((8, 8, rows), f32),
        V((8 * rows, rows), f32),
        V((3, 1, 16 * rows), f32),
        V((3, 1, 16 * rows), f32),
        V((1, 16 * rows), f32),
        V((16, 1, 16 * rows), f32),
        V((1, 16 * rows), f32),
        V((1, 16 * rows), f32),
        V((2, 8, e, rows), bf16),
        V((8, e, rows), bf16),
        V((8, e, rows), bf16),
        V((2, 2, e // 2, rows), bf16),
        V((2, 2, e, rows), bf16),
        V((2, e, rows), bf16),
        V((8, rows, e), bf16),
        V((2, 2, half, e), bf16),
        V((2, 2, rows, e), bf16),
        V((2, rows, e), bf16),
        V((2 * rows, e), bf16),
        V((2, 2, 2, 4, 4, half, rows), bf16),
        V((2, 2, 4, 4, half, rows), bf16),
        V((2, 2, 4, 4, half, rows), bf16),
        V((3, 2, 4, half, rows), bf16),
        V((3, 2, 4, half, rows), bf16),
        V((2, 4, half, rows), bf16),
        V((2, 4, half, rows), bf16),
        V((3, 2, half, rows), bf16),
        V((3, 2, half, rows), bf16),
        V((2, 2, half, rows), bf16),
        V((3, half, rows), bf16),
        V((2, e), f32),
        V((16, 2, e), f32),
        V((8, 2, e), f32),
        pltpu.SemaphoreType.DMA((copies,)),
        pltpu.SemaphoreType.DMA((copies,)),
        pltpu.SemaphoreType.DMA((9,)),
    ]
    shapes = (
        jax.ShapeDtypeStruct((rows, e), bf16),
        jax.ShapeDtypeStruct((rows, e), bf16),
        jax.ShapeDtypeStruct((half, rows), f32),
        jax.ShapeDtypeStruct((1, e), f32),
        jax.ShapeDtypeStruct((1, e), f32),
    )
    anywhere = pl.BlockSpec(memory_space=pl.ANY)
    results = pl.pallas_call(
        kernel,
        out_shape=shapes,
        in_specs=[anywhere] * 9,
        out_specs=(vmem,) * 5,
        scratch_shapes=scratch,
        compiler_params=pltpu.CompilerParams(
            collective_id=0, has_side_effects=True, vmem_limit_bytes=60 * 1024 * 1024
        ),
        cost_estimate=pl.CostEstimate(flops=16_000_000_000, bytes_accessed=5_000_000, transcendentals=2_100_000),
    )(
        q_hidden, d_hidden, positive.reshape(1, rows), query_part.reshape(1, rows), loss_weight.reshape(1, rows),
        doc_part.reshape(1, rows), norm_gain.reshape(1, e), norm_bias.reshape(1, e), proj,
    )
    dq, dd, d_proj, d_gain, d_bias = pl.pallas_call(
        hand_over,
        out_shape=shapes,
        in_specs=[vmem] * 5,
        out_specs=(vmem,) * 5,
        cost_estimate=pl.CostEstimate(flops=0, bytes_accessed=1_200_000, transcendentals=0),
    )(*results)
    return dq, dd, d_proj.T, d_gain.reshape(e), d_bias.reshape(e)


def solution(mesh):
    placed = (
        P(("pb", "dev"), None),
        P(("dev", "pb"), None),
        P(("pb", "dev")),
        P(("pb", "dev")),
        P(("dev", "pb")),
        P(("pb", "dev")),
        P(),
        P(),
        P(),
    )
    return jax.shard_map(
        per_device,
        mesh=mesh,
        in_specs=placed,
        out_specs=(P(("pb", "dev"), None), P(("dev", "pb"), None), P("pb", "dev"), P(), P()),
        check_vma=False,
    )
```

profile of v0, /device:TPU:0, one launch (start us, length us, event | category | flops | bytes accessed | tf_op | source)
XLA Modules:
  0.0 94.2 jit_solution(15308138710107909411)
XLA Ops:
  0.6 91.7 %shard_map.128 = (bf16[128,1024]{1,0:T(8,128)(2,1)}, bf16[128,1024]{1,0:T(8,128)(2,1)}, f32[64,128]{1,0:T(8,128)}, f32[1,1024]{1,0:T(1,128)}, f32[1,1024]{1,0:T(1,128)}) custom-call(bf16[128,1024]{1,0:T(8,128)(2,1)} %qh_hbm.1, bf16[128,1024]{1,0:T(8,128)(2,1)} %dh_hbm.1, s32[1,128]{1,0:T(1,128)} %bitcast.14, s32[1,128]{1,0:T(1,128)} %bitcast.15, ...), custom_call_target="tpu_custom_call" | custom-call | flops 16000000000 | bytes 5000000 | tf_op jit(solution)/shard_map/pallas_call | solution.py:551
  92.3 1.9 %shard_map.129 = (bf16[128,1024]{1,0:T(8,128)(2,1)}, bf16[128,1024]{1,0:T(8,128)(2,1)}, f32[64,128]{1,0:T(8,128)}, f32[1,1024]{1,0:T(1,128)}, f32[1,1024]{1,0:T(1,128)}) custom-call(bf16[128,1024]{1,0:T(8,128)(2,1)} %get-tuple-element.15.refs_0_, bf16[128,1024]{1,0:T(8,128)(2,1)} %get-tuple-element.16.refs_1_, f32[64,128]{1,0:T(8,128)} %get-tuple-element.17.refs_2_, ...), custom_call_target="tpu_custom_call" | custom-call | bytes 1200000 | tf_op jit(solution)/shard_map/pallas_call | solution.py:565
where the time goes:
time: 94.3 us; the launch traced here: 94.2 us
  Pallas kernels  93.5 us (99%)
    pallas_call x1, Pallas kernels, per_device(): pl.pallas_call(kernel, out_shape=shapes, in_specs=[anywhere] * 9, out_spe...  91.7 us

commit v1 on v0

--- a/solution.py
+++ b/solution.py
@@ -9,8 +9,8 @@
 f32, bf16 = jnp.float32, jnp.bfloat16
 MESH = pl.DeviceIdType.MESH
 rows, width = 128, 1024
-half = rows // 2
-copies = 160
+half, quarter = rows // 2, rows // 4
+copies = 200
 OFFSETS = ((0, 0), (1, 0), (0, 1), (0, 3), (0, 2), (1, 2), (1, 1), (1, 3))
 NT = (((1,), (1,)), ((), ()))
 
@@ -21,7 +21,7 @@
     qh, dh, pos_in, qpart_in, weight_in, dpart_in, gain, bias,
     proj, qbuf, dbuf, dt, st, gt, unit, normed, recip, inv, out_t, lab_q, lab_d, labs, dlab, dcol, mst, sst, lsend, lbuf,
     lsef, lrel, gqp, cbuf, sbuf, qfold, qring, qx, gdp, dfold, dring, dx_buf,
-    ge, hp, hc, hs, hz1, hy1, h0, h1, hy2, hz2, hx, hx3, gb, gba, gbb,
+    ge, gs, hs0, hs1, r0, r1, h0, h1, f0, f1, gb, gba, gbb,
     send_sem, recv_sem, local_sem,
 ):
     pb, dev = lax.axis_index("pb"), lax.axis_index("dev")
@@ -33,9 +33,6 @@
 
     def d_peer(dx, dz):
         return (lax.rem(z + dz, 4) * 2 + lax.rem(xl + dx, 2), y * 4 + lax.rem(xh + dx, 2) * 2 + core)
-
-    def x_peer(dh, dl):
-        return (z * 2 + lax.rem(xl + dl, 2), y * 4 + lax.rem(xh + dh, 2) * 2 + core)
 
     started = []
 
@@ -64,7 +61,7 @@
         loads.append(pltpu.make_async_copy(src, dst, local_sem.at[n]))
         loads[-1].start()
     barrier = pltpu.get_barrier_semaphore()
-    peers = [q_peer(*o) for o in q_offsets[1:]] + [d_peer(*o) for o in d_offsets[1:]] + [x_peer(1, 0)]
+    peers = [q_peer(*o) for o in q_offsets[1:]] + [d_peer(*o) for o in d_offsets[1:]]
     for peer in peers:
         pl.semaphore_signal(barrier, inc=1, device_id=peer, device_id_type=MESH)
 
@@ -88,7 +85,7 @@
     block = 8 * rows
 
     def q_at(core_index, k, offset=0):
-        return pl.multiple_of(core_index * block + k * rows + offset, half)
+        return pl.multiple_of(core_index * block + k * rows + offset, quarter)
 
     lab_copies = []
     for dx, dy, dc in q_offsets[1:]:
@@ -108,11 +105,11 @@
     qbuf[pl.ds(q_at(core, 0), rows), :] = u[:rows].astype(bf16)
     dbuf[0:rows, :] = u[rows:].astype(bf16)
 
-    def q_half(k, h):
-        return qbuf.at[pl.ds(q_at(core, k, h * half), half), :]
-
-    def d_half(k, h):
-        return dbuf.at[pl.ds(k * rows + h * half, half), :]
+    def q_part(k, first, count):
+        return qbuf.at[pl.ds(q_at(core, k, first * quarter), count * quarter), :]
+
+    def d_part(k, first, count):
+        return dbuf.at[pl.ds(k * rows + first * quarter, count * quarter), :]
 
     def to_sibling(k):
         part = qbuf.at[pl.ds(pl.multiple_of(core * block + k * rows, rows), rows), :]
@@ -120,35 +117,41 @@
 
     q_got, d_got, sib = {}, {}, {}
 
-    def hop(part, got, peer, k, h, to, way):
-        got[to, h] = send(part(k, h), part(to, h), peer(1, 0) if way == 0 else peer(0, way))
-
-    towers = ((q_half, q_got, q_peer), (d_half, d_got, d_peer))
-    for h in range(2):
+    def hop(part, got, peer, k, span, to, way):
+        got[to, span] = send(part(k, *span), part(to, *span), peer(1, 0) if way == 0 else peer(0, way))
+
+    towers = ((q_part, q_got, q_peer), (d_part, d_got, d_peer))
+    A, B, A0, A1, B0, B1 = (0, 2), (2, 2), (0, 1), (1, 1), (2, 1), (3, 1)
+    for spans in (((A, 3, 1), (B, 2, 3), (A0, 1, 0), (B0, 1, 0)), ((B, 3, 1), (A, 2, 3), (A1, 1, 0), (B1, 1, 0))):
         for tower in towers:
-            hop(*tower, 0, h, 3, 1)
-            hop(*tower, 0, 1 - h, 2, 3)
-            hop(*tower, 0, h, 1, 0)
+            for span, to, way in spans:
+                hop(*tower, 0, span, to, way)
     sib[0] = to_sibling(0)
-    out_t[...] = normal_out.T
+    out_t[:, 0 : 2 * rows] = normal_out.T
+    out_sib = send(out_t.at[:, pl.ds(0, 2 * rows)], out_t.at[:, pl.ds(2 * rows, 2 * rows)], q_peer(0, 0, 1))
     for tower in towers:
-        arrive(tower[1][3, 0])
-        hop(*tower, 3, 0, 4, 1)
-        arrive(tower[1][2, 1])
-        hop(*tower, 2, 1, 4, 3)
+        arrive(tower[1][1, A0])
+        hop(*tower, 1, A0, 7, 1)
     for tower in towers:
-        arrive(tower[1][1, 0])
-        hop(*tower, 1, 0, 7, 1)
+        arrive(tower[1][3, A])
+        hop(*tower, 3, A, 4, 1)
+        arrive(tower[1][2, B])
+        hop(*tower, 2, B, 4, 3)
     for tower in towers:
-        arrive(tower[1][1, 1])
-        hop(*tower, 1, 1, 6, 3)
-        hop(*tower, 1, 1, 7, 1)
-        hop(*tower, 1, 0, 6, 3)
+        arrive(tower[1][1, B0])
+        hop(*tower, 1, B0, 6, 3)
+        arrive(tower[1][1, A1])
+        hop(*tower, 1, A1, 7, 1)
+        arrive(tower[1][1, B1])
+        hop(*tower, 1, B1, 6, 3)
+    for tower in towers:
+        arrive(tower[1][3, B])
+        hop(*tower, 3, B, 7, 0)
+        arrive(tower[1][2, A])
+        hop(*tower, 2, A, 6, 0)
     sib[1] = to_sibling(1)
-    arrive(q_got[3, 1], q_got[2, 0])
     sib[2], sib[3] = to_sibling(2), to_sibling(3)
     arrive(*lab_copies)
-    arrive(d_got[3, 1], d_got[2, 0])
 
     for k in range(8):
         dcol[k * rows : (k + 1) * rows, :] = jnp.broadcast_to(dlab[k, 0:1, :], (rows, rows)).T
@@ -204,16 +207,17 @@
     arrive(sib[0], sib[1], sib[2], sib[3])
     scores(0, (0, 1, 2))
 
-    for tower in towers:
-        arrive(tower[1][7, 0])
-        hop(*tower, 7, 0, 5, 1)
-        arrive(tower[1][6, 1])
-        hop(*tower, 6, 1, 5, 3)
-    arrive(q_got[7, 1], q_got[6, 0])
+    for a, b in ((A0, B0), (A1, B1)):
+        for tower in towers:
+            arrive(tower[1][7, a])
+            hop(*tower, 7, a, 5, 1)
+            arrive(tower[1][6, b])
+            hop(*tower, 6, b, 5, 3)
+    arrive(q_got[4, A], q_got[4, B])
+    sib[4] = to_sibling(4)
+    arrive(q_got[7, B], q_got[6, A])
     sib[6], sib[7] = to_sibling(6), to_sibling(7)
-    arrive(q_got[4, 0], q_got[4, 1])
-    sib[4] = to_sibling(4)
-    arrive(d_got[7, 1], d_got[6, 0], d_got[4, 0], d_got[4, 1])
+    arrive(d_got[7, B], d_got[6, A], d_got[4, A], d_got[4, B])
     transpose_docs(6, 2)
     transpose_docs(4, 1)
     scores(2, (0, 1, 2))
@@ -221,9 +225,9 @@
     scores(0, (3, 1, 1))
     scores(2, (3, 1, 1))
 
-    arrive(q_got[5, 0], q_got[5, 1])
+    arrive(*(q_got[5, span] for span in (A0, B0, A1, B1)))
     sib[5] = to_sibling(5)
-    arrive(d_got[5, 0], d_got[5, 1])
+    arrive(*(d_got[5, span] for span in (A0, B0, A1, B1)))
     transpose_docs(5, 1)
     scores(1, (0, 1, 2))
     scores(1, (3, 1, 1))
@@ -238,20 +242,16 @@
     places = []
     for n in range(16):
         c, (dx, dy) = n // 8, OFFSETS[n % 8]
-        place = c * block + (lax.rem(y + dy, 4) * 2 + lax.rem(xl + dx, 2)) * rows
-        places.append(pl.ds(pl.multiple_of(place, rows), rows))
-        lsend[:, places[-1]] = local[:, n * rows : (n + 1) * rows]
+        places.append(c * 8 + lax.rem(y + dy, 4) * 2 + lax.rem(xl + dx, 2))
+        lsend[pl.ds(places[-1], 1), :] = local[:, n * rows : (n + 1) * rows]
     lse_copies = [send(lsend, lbuf.at[s], q_peer(*q_offsets[s])) for s in range(1, 16)]
     lbuf[0] = lsend[...]
     arrive(*lse_copies)
-    every = [lbuf[s] for s in range(16)]
-    top = every[0]
-    for e in every[1:]:
-        top = jnp.maximum(top, e)
-    total = sum(jnp.exp(e - top) for e in every)
-    lsef[...] = top + jnp.log(total)
+    every = lbuf[...]
+    top = jnp.max(every, axis=0)
+    lsef[...] = top + jnp.log(jnp.sum(jnp.exp(every - top[None]), axis=0))
     for n, place in enumerate(places):
-        lrel[:, n * rows : (n + 1) * rows] = lsef[:, place]
+        lrel[:, n * rows : (n + 1) * rows] = lsef[pl.ds(place, 1), :]
     for b in range(3):
         sst[b] = jnp.exp(mst[b] - lrel[...])
 
@@ -303,36 +303,45 @@
 
     slots = ((0, 2, 3, 4), (1, 6, 7, 5))
 
-    def far_terms(src, fold, ring, peer, h, dx):
+    def part_of(h, c, size):
+        return pl.ds((2 * c + h) * size, size)
+
+    def far_terms(src, fold, ring, peer, size, dx):
         far = slots[dx][3]
         return [
-            send(src.at[far, pl.ds(0, h), :], fold.at[dx, 0], peer(0, 1)),
-            send(src.at[far, pl.ds(h, h), :], fold.at[dx, 1], peer(0, 3)),
+            [send(src.at[far, part_of(h, c, size), :], fold.at[dx, h, c], peer(0, 3 if h else 1)) for h in range(2)]
+            for c in range(2)
         ]
 
-    def near_terms(src, fold, ring, peer, h, dx):
-        _, plus, minus, _ = slots[dx]
-        return [
-            send(src.at[plus, pl.ds(h, h), :], ring.at[dx, 0, pl.ds(h, h), :], peer(0, 1)),
-            send(src.at[minus, pl.ds(0, h), :], ring.at[dx, 1, pl.ds(0, h), :], peer(0, 3)),
-        ]
-
-    def merged(src, fold, ring, peer, h, dx, waits):
-        _, plus, minus, _ = slots[dx]
-        arrive(waits[0])
-        src[plus, 0:h, :] = (src[plus, 0:h, :].astype(f32) + fold[dx, 0].astype(f32)).astype(bf16)
-        a = send(src.at[plus, pl.ds(0, h), :], ring.at[dx, 0, pl.ds(0, h), :], peer(0, 1))
-        arrive(waits[1])
-        src[minus, h : 2 * h, :] = (src[minus, h : 2 * h, :].astype(f32) + fold[dx, 1].astype(f32)).astype(bf16)
-        b = send(src.at[minus, pl.ds(h, h), :], ring.at[dx, 1, pl.ds(h, h), :], peer(0, 3))
-        return [a, b]
-
-    def ring_sum(src, ring, dx, waits):
-        arrive(*waits)
-        return src[dx].astype(f32) + ring[dx, 0].astype(f32) + ring[dx, 1].astype(f32)
-
-    D = (gdp, dfold, dring, d_peer, half)
-    Q = (sbuf, qfold, qring, q_peer, width // 2)
+    def near_terms(src, fold, ring, peer, size, dx):
+        got = []
+        for c in range(2):
+            for h, way in ((1, 1), (0, 3)):
+                part = part_of(h, c, size)
+                got.append(send(src.at[slots[dx][1 if h else 2], part, :], ring.at[dx, 1 - h, part, :], peer(0, way)))
+        return got
+
+    def merged(src, fold, ring, peer, size, dx, c, waits):
+        got = []
+        for h in range(2):
+            k, part = slots[dx][1 + h], part_of(h, c, size)
+            rows_of = slice((2 * c + h) * size, (2 * c + h + 1) * size)
+            arrive(waits[c][h])
+            src[k, rows_of, :] = (src[k, rows_of, :].astype(f32) + fold[dx, h, c].astype(f32)).astype(bf16)
+            got.append(send(src.at[k, part, :], ring.at[dx, h, part, :], peer(0, 3 if h else 1)))
+        return got
+
+    def ring_sum(src, ring, dx, low, size):
+        span = slice(low, low + size)
+        return src[dx, span, :].astype(f32) + ring[dx, 0, span, :].astype(f32) + ring[dx, 1, span, :].astype(f32)
+
+    def across(src, ring, buf, peer, size, c):
+        span = pl.ds(c * 2 * size, 2 * size)
+        buf[0, c * 2 * size : (c + 1) * 2 * size, :] = ring_sum(src, ring, 1, c * 2 * size, 2 * size).astype(bf16)
+        return send(buf.at[0, span, :], buf.at[1, span, :], peer(1, 0))
+
+    D = (gdp, dfold, dring, d_peer, quarter)
+    Q = (sbuf, qfold, qring, q_peer, width // 4)
     query_terms(2, 1)
     query_terms(2, 0)
     query_terms(3, 1)
@@ -343,38 +352,55 @@
     query_terms(3, 0)
     both_cores(6)
     both_cores(7)
-    q_ring1 = near_terms(*Q, 1)
+    q_near1 = near_terms(*Q, 1)
     doc_terms(3)
-    d_ring1 = near_terms(*D, 1)
+    d_near1 = near_terms(*D, 1)
     both_cores(4)
     query_terms(1, 1)
     query_terms(0, 1)
     query_terms(1, 0)
-    d_ring1 += merged(*D, 1, d_fold1)
+    d_ring1 = [merged(*D, 1, 0, d_fold1)]
+    q_ring1 = [merged(*Q, 1, 0, q_fold1)]
+    d_ring1.append(merged(*D, 1, 1, d_fold1))
+    q_ring1.append(merged(*Q, 1, 1, q_fold1))
     d_fold0 = far_terms(*D, 0)
-    q_ring1 += merged(*Q, 1, q_fold1)
     q_fold0 = far_terms(*Q, 0)
     doc_terms(1)
-    d_ring0 = near_terms(*D, 0)
+    d_near0 = near_terms(*D, 0)
     both_cores(2)
     both_cores(3)
-    q_ring0 = near_terms(*Q, 0)
+    q_near0 = near_terms(*Q, 0)
+    doc_terms(0)
     query_terms(0, 0)
-    doc_terms(0)
     both_cores(1)
     both_cores(0)
-    dx_buf[0] = ring_sum(gdp, dring, 1, d_ring1).astype(bf16)
-    d_across = send(dx_buf.at[0], dx_buf.at[1], d_peer(1, 0))
-    qx[0] = ring_sum(sbuf, qring, 1, q_ring1).astype(bf16)
-    q_across = send(qx.at[0], qx.at[1], q_peer(1, 0))
-    d_ring0 += merged(*D, 0, d_fold0)
-    q_ring0 += merged(*Q, 0, q_fold0)
+    d_across, q_across = [], []
+    arrive(*d_near1, *q_near1)
+    for c in range(2):
+        arrive(*d_ring1[c])
+        d_across.append(across(gdp, dring, dx_buf, d_peer, quarter, c))
+        arrive(*q_ring1[c])
+        q_across.append(across(sbuf, qring, qx, q_peer, width // 4, c))
+    d_ring0, q_ring0 = [], []
+    for c in range(2):
+        d_ring0 += merged(*D, 0, c, d_fold0)
+        q_ring0 += merged(*Q, 0, c, q_fold0)
+
+    left = lax.broadcasted_iota(jnp.int32, (rows, rows), 1) < half
+    ge_copies = []
 
     def backward(g_unit, low, out):
         span = slice(low, low + rows)
         uu, nn = unit[span, :], normed[span, :]
-        g = ((g_unit - uu * jnp.sum(uu * g_unit, axis=1, keepdims=True)) * inv[span, :]).astype(bf16)
-        ge[span, :] = g
+        g = (g_unit - uu * jnp.sum(uu * g_unit, axis=1, keepdims=True)) * inv[span, :]
+        for j in range(4):
+            b0, b1 = g[:, 2 * j * rows : (2 * j + 1) * rows], g[:, (2 * j + 1) * rows : (2 * j + 2) * rows]
+            n0 = jnp.where(left, b0, pltpu.roll(b1, half, 1))
+            n1 = jnp.where(left, pltpu.roll(b0, half, 1), b1)
+            ge[span, j * rows : (j + 1) * rows] = jnp.where(core == 0, n0, n1).astype(bf16)
+            gs[span, j * rows : (j + 1) * rows] = jnp.where(core == 0, n1, n0).astype(bf16)
+        ge_copies.append(send(gs.at[pl.ds(low, rows), :], ge.at[pl.ds(2 * rows + low, rows), :], q_peer(0, 0, 1)))
+        g = g.astype(bf16)
         gn = lax.dot_general(g, proj[...], NT, preferred_element_type=f32)
         scaled = gn * gain[...]
         out[...] = (
@@ -383,13 +409,11 @@
         ).astype(bf16)
         return jnp.sum(gn * nn, axis=0, keepdims=True), jnp.sum(gn, axis=0, keepdims=True)
 
-    g_doc = ring_sum(gdp, dring, 0, d_ring0)
-    arrive(d_across)
-    g_doc = logit_scale * (g_doc + dx_buf[1].astype(f32))
-    g_query = ring_sum(sbuf, qring, 0, q_ring0)
-    arrive(q_across)
+    arrive(*d_near0, *d_ring0, *d_across)
+    g_doc = logit_scale * (ring_sum(gdp, dring, 0, 0, rows) + dx_buf[1].astype(f32))
     gain_d, bias_d = backward(g_doc, rows, dd)
-    gain_q, bias_q = backward(logit_scale * (g_query + qx[1].astype(f32)).T, 0, dq)
+    arrive(*q_near0, *q_ring0, *q_across)
+    gain_q, bias_q = backward(logit_scale * (ring_sum(sbuf, qring, 0, 0, width) + qx[1].astype(f32)).T, 0, dq)
 
     gb[0:1, :] = gain_d + gain_q
     gb[1:2, :] = bias_d + bias_q
@@ -397,37 +421,32 @@
     gb_copies = [send(gb, gba.at[order], q_peer(*o)) for o in q_offsets[1:]]
     gba[order] = gb[...]
 
-    left = lax.broadcasted_iota(jnp.int32, (half, rows), 1) < half
+    low_left = left[:half]
+    arrive(out_sib, *ge_copies)
 
     def head(n, carry):
         for a in range(2):
             v = jnp.dot(
                 out_t[pl.ds(pl.multiple_of((2 * n + a) * rows, rows), rows), :], ge[...], preferred_element_type=f32
             )
-            for j in range(8):
+            for j in range(4):
                 upper, lower = v[:half, j * rows : (j + 1) * rows], v[half:, j * rows : (j + 1) * rows]
-                hp[0, a, j % 2, j // 2, n] = jnp.where(left, upper, pltpu.roll(lower, half, 1)).astype(bf16)
-                hp[1, a, j % 2, j // 2, n] = jnp.where(left, pltpu.roll(upper, half, 1), lower).astype(bf16)
+                for b in range(2):
+                    if b == 0:
+                        w = jnp.where(low_left, upper, pltpu.roll(lower, half, 1)).astype(bf16)
+                    else:
+                        w = jnp.where(low_left, pltpu.roll(upper, half, 1), lower).astype(bf16)
+                    hs0[b, n, a, j] = w[:quarter]
+                    hs1[(a + b) % 2, j, b, n] = w[quarter:]
         return carry
 
     lax.fori_loop(0, 4, head, 0)
-    head_core = [send(hp.at[1 - core, a], hc.at[a], q_peer(0, 0, 1)) for a in range(2)]
-    first = []
-    for a in range(2):
-        arrive(head_core[a])
-
-        def add_cores(n, carry):
-            for b in range(2):
-                hs[a, b, n] = (hp[core, a, b, n].astype(f32) + hc[a, b, n].astype(f32)).astype(bf16)
-            return carry
-
-        lax.fori_loop(0, 4, add_cores, 0)
-        for s in range(1, 4):
-            zz, yy = lax.rem(z + s, 4), lax.rem(y + s, 4)
-            if a == 0:
-                first.append(send(hs.at[0, :, :, zz], hz1.at[s - 1], d_peer(0, s)))
-            else:
-                first.append(send(hs.at[1, :, yy], hy1.at[s - 1], q_peer(0, s)))
+    diagonal = lax.rem(xl + xh, 2)
+    first0, first1 = [], []
+    for s, (dx, dz) in enumerate(d_offsets[1:]):
+        first0.append(send(hs0.at[lax.rem(xh + dx, 2), lax.rem(z + dz, 4)], r0.at[s], d_peer(dx, dz)))
+        dy = dz
+        first1.append(send(hs1.at[lax.rem(diagonal + dx, 2), lax.rem(y + dy, 4)], r1.at[s], q_peer(dx, dy)))
 
     arrive(*gb_copies)
     acc = gba[0]
@@ -438,23 +457,22 @@
     gb_copies = [send(gbb.at[order], gbb.at[order], d_peer(*o)) for o in d_offsets[1:]]
 
     def total_of(own, got):
-        return own.astype(f32) + sum(got[n].astype(f32) for n in range(3))
-
-    arrive(*first[:3])
-    h0[...] = total_of(hs[0, :, :, z], hz1).astype(bf16)
-    second = [send(h0.at[:, lax.rem(y + s, 4)], hy2.at[s - 1], q_peer(0, s)) for s in range(1, 4)]
-    arrive(*first[3:])
-    h1[...] = total_of(hs[1, :, y], hy1).astype(bf16)
-    second += [send(h1.at[:, lax.rem(z + s, 4)], hz2.at[s - 1], d_peer(0, s)) for s in range(1, 4)]
-    arrive(*second)
-    hx[0] = total_of(h0[:, y], hy2).astype(bf16)
-    hx[1] = total_of(h1[:, z], hz2).astype(bf16)
-    third = []
-    for s, (sh, sl) in enumerate(((0, 1), (1, 0), (1, 1))):
-        src = hx.at[lax.rem(xl + sl, 2), lax.rem(xh + sh, 2)]
-        third.append(send(src, hx3.at[s], x_peer(sh, sl)))
-    arrive(*third)
-    final = total_of(hx[xl, xh], hx3)
+        return own.astype(f32) + sum(got[n].astype(f32) for n in range(7))
+
+    arrive(*first0)
+    h0[...] = total_of(hs0[xh, z], r0).astype(bf16)
+    second0 = [
+        send(h0.at[lax.rem(xl + dx, 2), lax.rem(y + dy, 4)], f0.at[s], q_peer(dx, dy))
+        for s, (dx, dy) in enumerate(d_offsets[1:])
+    ]
+    arrive(*first1)
+    h1[...] = total_of(hs1[diagonal, y], r1).astype(bf16)
+    second1 = [
+        send(h1.at[lax.rem(xh + dx, 2), lax.rem(z + dz, 4)], f1.at[s], d_peer(dx, dz))
+        for s, (dx, dz) in enumerate(d_offsets[1:])
+    ]
+    arrive(*second0, *second1)
+    final = jnp.concatenate([total_of(h0[xl, y], f0), total_of(h1[xh, z], f1)], axis=0)
     dproj[:, 0:half] = final[:, :half].T
     dproj[:, half:rows] = final[:, half:].T
 
@@ -499,7 +517,7 @@
         V((2 * rows, e), f32),
         V((2 * rows, 1), f32),
         V((2 * rows, 1), f32),
-        V((e, 2 * rows), bf16),
+        V((e, 4 * rows), bf16),
         V((8, rows), f32),
         V((8, rows), f32),
         V((8, 16 * rows), f32),
@@ -507,32 +525,30 @@
         V((8 * rows, rows), f32),
         V((3, 1, 16 * rows), f32),
         V((3, 1, 16 * rows), f32),
-        V((1, 16 * rows), f32),
-        V((16, 1, 16 * rows), f32),
-        V((1, 16 * rows), f32),
+        V((16, rows), f32),
+        V((16, 16, rows), f32),
+        V((16, rows), f32),
         V((1, 16 * rows), f32),
         V((2, 8, e, rows), bf16),
         V((8, e, rows), bf16),
         V((8, e, rows), bf16),
-        V((2, 2, e // 2, rows), bf16),
+        V((2, 2, 2, e // 4, rows), bf16),
         V((2, 2, e, rows), bf16),
         V((2, e, rows), bf16),
         V((8, rows, e), bf16),
-        V((2, 2, half, e), bf16),
+        V((2, 2, 2, quarter, e), bf16),
         V((2, 2, rows, e), bf16),
         V((2, rows, e), bf16),
-        V((2 * rows, e), bf16),
-        V((2, 2, 2, 4, 4, half, rows), bf16),
-        V((2, 2, 4, 4, half, rows), bf16),
-        V((2, 2, 4, 4, half, rows), bf16),
-        V((3, 2, 4, half, rows), bf16),
-        V((3, 2, 4, half, rows), bf16),
-        V((2, 4, half, rows), bf16),
-        V((2, 4, half, rows), bf16),
-        V((3, 2, half, rows), bf16),
-        V((3, 2, half, rows), bf16),
-        V((2, 2, half, rows), bf16),
-        V((3, half, rows), bf16),
+        V((4 * rows, 4 * rows), bf16),
+        V((2 * rows, 4 * rows), bf16),
+        V((2, 4, 2, 4, quarter, rows), bf16),
+        V((2, 4, 2, 4, quarter, rows), bf16),
+        V((7, 2, 4, quarter, rows), bf16),
+        V((7, 2, 4, quarter, rows), bf16),
+        V((2, 4, quarter, rows), bf16),
+        V((2, 4, quarter, rows), bf16),
+        V((7, quarter, rows), bf16),
+        V((7, quarter, rows), bf16),
         V((2, e), f32),
         V((16, 2, e), f32),
         V((8, 2, e), f32),

time: 94.3 us -> 90 us (0.954)
  Pallas kernels: 93.5 us -> 89.2 us
    pallas_call x1, Pallas kernels: 91.7 us -> 87.3 us  [per_device(): pl.pallas_call(kernel, out_shape=shapes, in_specs=[anywhere] * 9, out_spe...]
where the time goes in v1:
time: 90 us; the launch traced here: 89.8 us
  Pallas kernels  89.2 us (99%)
    pallas_call x1, Pallas kernels, per_device(): pl.pallas_call(kernel, out_shape=shapes, in_specs=[anywhere] * 9, out_spe...  87.3 us
    pallas_call x1, Pallas kernels, per_device(): pl.pallas_call(hand_over, out_shape=shapes, in_specs=[vmem] * 5, out_spec...  1.85 us

profile of v1, /device:TPU:0, one launch (start us, length us, event | category | flops | bytes accessed | tf_op | source)
XLA Modules:
  0.0 89.8 jit_solution(16936255516984367897)
XLA Ops:
  0.6 87.3 %shard_map.128 = (bf16[128,1024]{1,0:T(8,128)(2,1)}, bf16[128,1024]{1,0:T(8,128)(2,1)}, f32[64,128]{1,0:T(8,128)}, f32[1,1024]{1,0:T(1,128)}, f32[1,1024]{1,0:T(1,128)}) custom-call(bf16[128,1024]{1,0:T(8,128)(2,1)} %qh_hbm.1, bf16[128,1024]{1,0:T(8,128)(2,1)} %dh_hbm.1, s32[1,128]{1,0:T(1,128)} %bitcast.14, s32[1,128]{1,0:T(1,128)} %bitcast.15, ...), custom_call_target="tpu_custom_call" | custom-call | flops 16000000000 | bytes 5000000 | tf_op jit(solution)/shard_map/pallas_call | solution.py:567
  88.0 1.9 %shard_map.129 = (bf16[128,1024]{1,0:T(8,128)(2,1)}, bf16[128,1024]{1,0:T(8,128)(2,1)}, f32[64,128]{1,0:T(8,128)}, f32[1,1024]{1,0:T(1,128)}, f32[1,1024]{1,0:T(1,128)}) custom-call(bf16[128,1024]{1,0:T(8,128)(2,1)} %get-tuple-element.15.refs_0_, bf16[128,1024]{1,0:T(8,128)(2,1)} %get-tuple-element.16.refs_1_, f32[64,128]{1,0:T(8,128)} %get-tuple-element.17.refs_2_, ...), custom_call_target="tpu_custom_call" | custom-call | bytes 1200000 | tf_op jit(solution)/shard_map/pallas_call | solution.py:581

commit v2 on v1

--- a/solution.py
+++ b/solution.py
@@ -21,7 +21,7 @@
     qh, dh, pos_in, qpart_in, weight_in, dpart_in, gain, bias,
     proj, qbuf, dbuf, dt, st, gt, unit, normed, recip, inv, out_t, lab_q, lab_d, labs, dlab, dcol, mst, sst, lsend, lbuf,
     lsef, lrel, gqp, cbuf, sbuf, qfold, qring, qx, gdp, dfold, dring, dx_buf,
-    ge, gs, hs0, hs1, r0, r1, h0, h1, f0, f1, gb, gba, gbb,
+    ge, gs, gns, hs0, hs1, r0, r1, h0, h1, f0, f1, gb, gba, gbb,
     send_sem, recv_sem, local_sem,
 ):
     pb, dev = lax.axis_index("pb"), lax.axis_index("dev")
@@ -87,6 +87,36 @@
     def q_at(core_index, k, offset=0):
         return pl.multiple_of(core_index * block + k * rows + offset, quarter)
 
+    embed = jnp.dot(normal_out, proj[...], preferred_element_type=f32)
+    i = lax.rsqrt(jnp.sum(embed * embed, axis=1, keepdims=True) + 1e-06)
+    inv[...] = i
+    u = embed * i
+    unit[...] = u
+    qbuf[pl.ds(q_at(core, 0), rows), :] = u[:rows].astype(bf16)
+    dbuf[0:rows, :] = u[rows:].astype(bf16)
+
+    def q_part(k, first, count):
+        return qbuf.at[pl.ds(q_at(core, k, first * quarter), count * quarter), :]
+
+    def d_part(k, first, count):
+        return dbuf.at[pl.ds(k * rows + first * quarter, count * quarter), :]
+
+    def to_sibling(k):
+        part = qbuf.at[pl.ds(pl.multiple_of(core * block + k * rows, rows), rows), :]
+        return send(part, part, q_peer(0, 0, 1))
+
+    q_got, d_got, sib = {}, {}, {}
+
+    def hop(part, got, peer, k, span, to, way):
+        got[to, span] = send(part(k, *span), part(to, *span), peer(1, 0) if way == 0 else peer(0, way))
+
+    towers = ((q_part, q_got, q_peer), (d_part, d_got, d_peer))
+    A, B, A0, A1, B0, B1 = (0, 2), (2, 2), (0, 1), (1, 1), (2, 1), (3, 1)
+    for spans in (((A, 3, 1), (B, 2, 3), (A0, 1, 0), (B0, 1, 0)), ((B, 3, 1), (A, 2, 3), (A1, 1, 0), (B1, 1, 0))):
+        for tower in towers:
+            for span, to, way in spans:
+                hop(*tower, 0, span, to, way)
+    sib[0] = to_sibling(0)
     lab_copies = []
     for dx, dy, dc in q_offsets[1:]:
         k = OFFSETS.index((dx, (4 - dy) % 4))
@@ -96,37 +126,6 @@
         lab_copies.append(send(lab_d, dlab.at[OFFSETS.index((dx, (4 - dz) % 4))], d_peer(dx, dz)))
     labs[:, pl.ds(pl.multiple_of(core * block, rows), rows)] = lab_q[...]
     dlab[0] = lab_d[...]
-
-    embed = jnp.dot(normal_out, proj[...], preferred_element_type=f32)
-    i = lax.rsqrt(jnp.sum(embed * embed, axis=1, keepdims=True) + 1e-06)
-    inv[...] = i
-    u = embed * i
-    unit[...] = u
-    qbuf[pl.ds(q_at(core, 0), rows), :] = u[:rows].astype(bf16)
-    dbuf[0:rows, :] = u[rows:].astype(bf16)
-
-    def q_part(k, first, count):
-        return qbuf.at[pl.ds(q_at(core, k, first * quarter), count * quarter), :]
-
-    def d_part(k, first, count):
-        return dbuf.at[pl.ds(k * rows + first * quarter, count * quarter), :]
-
-    def to_sibling(k):
-        part = qbuf.at[pl.ds(pl.multiple_of(core * block + k * rows, rows), rows), :]
-        return send(part, part, q_peer(0, 0, 1))
-
-    q_got, d_got, sib = {}, {}, {}
-
-    def hop(part, got, peer, k, span, to, way):
-        got[to, span] = send(part(k, *span), part(to, *span), peer(1, 0) if way == 0 else peer(0, way))
-
-    towers = ((q_part, q_got, q_peer), (d_part, d_got, d_peer))
-    A, B, A0, A1, B0, B1 = (0, 2), (2, 2), (0, 1), (1, 1), (2, 1), (3, 1)
-    for spans in (((A, 3, 1), (B, 2, 3), (A0, 1, 0), (B0, 1, 0)), ((B, 3, 1), (A, 2, 3), (A1, 1, 0), (B1, 1, 0))):
-        for tower in towers:
-            for span, to, way in spans:
-                hop(*tower, 0, span, to, way)
-    sib[0] = to_sibling(0)
     out_t[:, 0 : 2 * rows] = normal_out.T
     out_sib = send(out_t.at[:, pl.ds(0, 2 * rows)], out_t.at[:, pl.ds(2 * rows, 2 * rows)], q_peer(0, 0, 1))
     for tower in towers:
@@ -160,16 +159,18 @@
         for k in range(first, first + count):
             dt[:, k * rows : (k + 1) * rows] = dbuf[k * rows : (k + 1) * rows, :].T
 
-    lane = lax.broadcasted_iota(jnp.int32, (rows, 2 * rows), 0).astype(f32)
+    def lane(wide):
+        return lax.broadcasted_iota(jnp.int32, (rows, wide), 0).astype(f32)
 
     def bases(k):
         to_pb, to_dev = d_peer(*OFFSETS[k])
         return ((to_dev * 8 + to_pb) * rows).astype(f32)
 
-    def pair_cols(core_index, m):
-        return pl.ds(pl.multiple_of(core_index * block + m * 2 * rows, 2 * rows), 2 * rows)
+    def pair_cols(core_index, m, count=1):
+        return pl.ds(pl.multiple_of(core_index * block + m * 2 * rows, 2 * rows), count * 2 * rows)
 
     def score(first, count, piece, cols):
+        wide = cols.size
         s = logit_scale * lax.dot_general(
             dbuf[first * rows : (first + count) * rows, :], qbuf[cols, :], NT, preferred_element_type=f32
         )
@@ -177,13 +178,13 @@
         masked = []
         for n in range(count):
             k = first + n
-            col = dcol[k * rows : (k + 1) * rows, :]
-            valid = jnp.logical_or(part != jnp.concatenate([col, col], axis=1), lane == pos - bases(k))
+            col = jnp.concatenate([dcol[k * rows : (k + 1) * rows, :]] * (wide // rows), axis=1)
+            valid = jnp.logical_or(part != col, lane(wide) == pos - bases(k))
             masked.append(jnp.where(valid, s[n * rows : (n + 1) * rows], jnp.float32(-1e30)))
-        top = jnp.full((1, 2 * rows), -1e4, f32)
+        top = jnp.full((1, wide), -1e4, f32)
         for m in masked:
             top = jnp.maximum(top, jnp.max(m, axis=0, keepdims=True))
-        total = jnp.zeros((1, 2 * rows), f32)
+        total = jnp.zeros((1, wide), f32)
         for n, m in enumerate(masked):
             p = jnp.exp(m - top)
             total = total + jnp.sum(p, axis=0, keepdims=True)
@@ -193,19 +194,17 @@
 
     pieces = ((0, 4), (4, 2), (6, 2))
 
-    def scores(piece, pairs):
-        low, step, count = pairs
-
-        def body(n, carry):
-            m, c = low + step * (n // 2), lax.rem(n, 2)
-            score(*pieces[piece], piece, pair_cols(c, m))
+    def scores(piece, m, count):
+        def body(c, carry):
+            score(*pieces[piece], piece, pair_cols(c, m, count))
             return carry
 
-        lax.fori_loop(0, 2 * count, body, 0)
+        lax.fori_loop(0, 2, body, 0)
 
     transpose_docs(0, 4)
     arrive(sib[0], sib[1], sib[2], sib[3])
-    scores(0, (0, 1, 2))
+    scores(0, 0, 1)
+    scores(0, 1, 1)
 
     for a, b in ((A0, B0), (A1, B1)):
         for tower in towers:
@@ -220,21 +219,20 @@
     arrive(d_got[7, B], d_got[6, A], d_got[4, A], d_got[4, B])
     transpose_docs(6, 2)
     transpose_docs(4, 1)
-    scores(2, (0, 1, 2))
+    scores(2, 0, 2)
     arrive(sib[6], sib[7])
-    scores(0, (3, 1, 1))
-    scores(2, (3, 1, 1))
+    scores(0, 3, 1)
+    scores(2, 3, 1)
 
     arrive(*(q_got[5, span] for span in (A0, B0, A1, B1)))
     sib[5] = to_sibling(5)
     arrive(*(d_got[5, span] for span in (A0, B0, A1, B1)))
     transpose_docs(5, 1)
-    scores(1, (0, 1, 2))
-    scores(1, (3, 1, 1))
+    scores(1, 0, 2)
     arrive(sib[4], sib[5])
-    scores(0, (2, 1, 1))
-    scores(1, (2, 1, 1))
-    scores(2, (2, 1, 1))
+    scores(1, 2, 2)
+    scores(0, 2, 1)
+    scores(2, 2, 1)
 
     top = jnp.maximum(jnp.maximum(mst[0], mst[1]), mst[2])
     total = sum(sst[b] * jnp.exp(mst[b] - top) for b in range(3))
@@ -255,21 +253,27 @@
     for b in range(3):
         sst[b] = jnp.exp(mst[b] - lrel[...])
 
-    def grads(g, carry):
-        cols = pl.ds(pl.multiple_of(g * 2 * rows, 2 * rows), 2 * rows)
+    def grads(c, m, ks):
+        cols = pair_cols(c, m)
         pos, weight = labs[0:1, cols], labs[2:3, cols]
-        for k in range(8):
+        for k in ks:
             scale = sst[0 if k < 4 else 1 if k < 6 else 2, :, cols]
-            hit = jnp.where(lane == pos - bases(k), jnp.float32(1), jnp.float32(0))
+            hit = jnp.where(lane(2 * rows) == pos - bases(k), jnp.float32(1), jnp.float32(0))
             prob = st[k * rows : (k + 1) * rows, cols] * scale
             gt[k * rows : (k + 1) * rows, cols] = (weight * (prob - hit)).astype(bf16)
-        return carry
-
-    lax.fori_loop(0, 8, grads, 0)
+
+    def grads_of(ms, ks):
+        def body(c, carry):
+            for m in ms:
+                grads(c, m, ks)
+            return carry
+
+        lax.fori_loop(0, 2, body, 0)
+
 
     def doc_terms(m):
         def body(j, carry):
-            cols = pl.ds(pl.multiple_of(j * 256, 256), 256)
+            cols = pl.ds(pl.multiple_of(j * 512, 512), 512)
             v = jnp.dot(
                 gt[2 * m * rows : 2 * (m + 1) * rows, :], qbuf[:, cols], preferred_element_type=f32
             ).astype(bf16)
@@ -277,21 +281,16 @@
             gdp[2 * m + 1, :, cols] = v[rows:]
             return carry
 
-        lax.fori_loop(0, 4, body, 0)
+        lax.fori_loop(0, 2, body, 0)
 
     cores = {}
 
     def query_terms(m, other):
         cols = pair_cols(1 - core if other else core, m)
 
-        def body(j, carry):
-            part = pl.ds(pl.multiple_of(j * 512, 512), 512)
-            v = jnp.dot(dt[part, :], gt[:, cols], preferred_element_type=f32).astype(bf16)
-            gqp[other, 2 * m, part, :] = v[:, :rows]
-            gqp[other, 2 * m + 1, part, :] = v[:, rows:]
-            return carry
-
-        lax.fori_loop(0, 2, body, 0)
+        v = jnp.dot(dt[...], gt[:, cols], preferred_element_type=f32).astype(bf16)
+        gqp[other, 2 * m] = v[:, :rows]
+        gqp[other, 2 * m + 1] = v[:, rows:]
         if other:
             span = pl.ds(2 * m, 2)
             cores[m] = send(gqp.at[1, span], cbuf.at[span], q_peer(0, 0, 1))
@@ -342,31 +341,36 @@
 
     D = (gdp, dfold, dring, d_peer, quarter)
     Q = (sbuf, qfold, qring, q_peer, width // 4)
+    grads_of((2,), range(8))
     query_terms(2, 1)
     query_terms(2, 0)
-    query_terms(3, 1)
+    grads_of((0, 1, 3), (4, 5))
     doc_terms(2)
     d_fold1 = far_terms(*D, 1)
     both_cores(5)
     q_fold1 = far_terms(*Q, 1)
+    grads_of((3,), (0, 1, 2, 3, 6, 7))
+    query_terms(3, 1)
+    grads_of((0, 1), (6, 7))
+    doc_terms(3)
+    d_near1 = near_terms(*D, 1)
     query_terms(3, 0)
     both_cores(6)
     both_cores(7)
     q_near1 = near_terms(*Q, 1)
-    doc_terms(3)
-    d_near1 = near_terms(*D, 1)
     both_cores(4)
+    grads_of((0, 1), (0, 1, 2, 3))
     query_terms(1, 1)
-    query_terms(0, 1)
-    query_terms(1, 0)
     d_ring1 = [merged(*D, 1, 0, d_fold1)]
     q_ring1 = [merged(*Q, 1, 0, q_fold1)]
     d_ring1.append(merged(*D, 1, 1, d_fold1))
     q_ring1.append(merged(*Q, 1, 1, q_fold1))
     d_fold0 = far_terms(*D, 0)
     q_fold0 = far_terms(*Q, 0)
+    query_terms(0, 1)
     doc_terms(1)
     d_near0 = near_terms(*D, 0)
+    query_terms(1, 0)
     both_cores(2)
     both_cores(3)
     q_near0 = near_terms(*Q, 0)
@@ -386,43 +390,32 @@
         d_ring0 += merged(*D, 0, c, d_fold0)
         q_ring0 += merged(*Q, 0, c, q_fold0)
 
-    left = lax.broadcasted_iota(jnp.int32, (rows, rows), 1) < half
-    ge_copies = []
-
-    def backward(g_unit, low, out):
-        span = slice(low, low + rows)
-        uu, nn = unit[span, :], normed[span, :]
-        g = (g_unit - uu * jnp.sum(uu * g_unit, axis=1, keepdims=True)) * inv[span, :]
-        for j in range(4):
-            b0, b1 = g[:, 2 * j * rows : (2 * j + 1) * rows], g[:, (2 * j + 1) * rows : (2 * j + 2) * rows]
-            n0 = jnp.where(left, b0, pltpu.roll(b1, half, 1))
-            n1 = jnp.where(left, pltpu.roll(b0, half, 1), b1)
-            ge[span, j * rows : (j + 1) * rows] = jnp.where(core == 0, n0, n1).astype(bf16)
-            gs[span, j * rows : (j + 1) * rows] = jnp.where(core == 0, n1, n0).astype(bf16)
-        ge_copies.append(send(gs.at[pl.ds(low, rows), :], ge.at[pl.ds(2 * rows + low, rows), :], q_peer(0, 0, 1)))
-        g = g.astype(bf16)
-        gn = lax.dot_general(g, proj[...], NT, preferred_element_type=f32)
-        scaled = gn * gain[...]
-        out[...] = (
-            recip[span, :]
-            * (scaled - jnp.mean(scaled, axis=1, keepdims=True) - nn * jnp.mean(scaled * nn, axis=1, keepdims=True))
-        ).astype(bf16)
-        return jnp.sum(gn * nn, axis=0, keepdims=True), jnp.sum(gn, axis=0, keepdims=True)
-
+    left = lax.broadcasted_iota(jnp.int32, (2 * rows, rows), 1) < half
     arrive(*d_near0, *d_ring0, *d_across)
-    g_doc = logit_scale * (ring_sum(gdp, dring, 0, 0, rows) + dx_buf[1].astype(f32))
-    gain_d, bias_d = backward(g_doc, rows, dd)
+    g_doc = ring_sum(gdp, dring, 0, 0, rows) + dx_buf[1].astype(f32)
     arrive(*q_near0, *q_ring0, *q_across)
-    gain_q, bias_q = backward(logit_scale * (ring_sum(sbuf, qring, 0, 0, width) + qx[1].astype(f32)).T, 0, dq)
-
-    gb[0:1, :] = gain_d + gain_q
-    gb[1:2, :] = bias_d + bias_q
+    g_query = (ring_sum(sbuf, qring, 0, 0, width) + qx[1].astype(f32)).T
+    g_unit = logit_scale * jnp.concatenate([g_query, g_doc], axis=0)
+    uu = unit[...]
+    g = (g_unit - uu * jnp.sum(uu * g_unit, axis=1, keepdims=True)) * inv[...]
+    for j in range(4):
+        b0, b1 = g[:, 2 * j * rows : (2 * j + 1) * rows], g[:, (2 * j + 1) * rows : (2 * j + 2) * rows]
+        n0 = jnp.where(left, b0, pltpu.roll(b1, half, 1))
+        n1 = jnp.where(left, pltpu.roll(b0, half, 1), b1)
+        ge[0 : 2 * rows, j * rows : (j + 1) * rows] = jnp.where(core == 0, n0, n1).astype(bf16)
+        gs[:, j * rows : (j + 1) * rows] = jnp.where(core == 0, n1, n0).astype(bf16)
+    ge_copy = send(gs, ge.at[pl.ds(2 * rows, 2 * rows), :], q_peer(0, 0, 1))
+    gn = lax.dot_general(g.astype(bf16), proj[...], NT, preferred_element_type=f32)
+    nn = normed[...]
+    gns[...] = gn
+    gb[0:1, :] = jnp.sum(gn * nn, axis=0, keepdims=True)
+    gb[1:2, :] = jnp.sum(gn, axis=0, keepdims=True)
     order = (y * 2 + xl) * 2 + core
     gb_copies = [send(gb, gba.at[order], q_peer(*o)) for o in q_offsets[1:]]
     gba[order] = gb[...]
 
     low_left = left[:half]
-    arrive(out_sib, *ge_copies)
+    arrive(out_sib, ge_copy)
 
     def head(n, carry):
         for a in range(2):
@@ -447,6 +440,13 @@
         first0.append(send(hs0.at[lax.rem(xh + dx, 2), lax.rem(z + dz, 4)], r0.at[s], d_peer(dx, dz)))
         dy = dz
         first1.append(send(hs1.at[lax.rem(diagonal + dx, 2), lax.rem(y + dy, 4)], r1.at[s], q_peer(dx, dy)))
+    gn, nn = gns[...], normed[...]
+    scaled = gn * gain[...]
+    grad_h = recip[...] * (
+        scaled - jnp.mean(scaled, axis=1, keepdims=True) - nn * jnp.mean(scaled * nn, axis=1, keepdims=True)
+    )
+    dq[...] = grad_h[:rows].astype(bf16)
+    dd[...] = grad_h[rows:].astype(bf16)
 
     arrive(*gb_copies)
     acc = gba[0]
@@ -541,6 +541,7 @@
         V((2, rows, e), bf16),
         V((4 * rows, 4 * rows), bf16),
         V((2 * rows, 4 * rows), bf16),
+        V((2 * rows, e), f32),
         V((2, 4, 2, 4, quarter, rows), bf16),
         V((2, 4, 2, 4, quarter, rows), bf16),
         V((7, 2, 4, quarter, rows), bf16),

time: 90 us -> 87.1 us (0.968)
  Pallas kernels: 89.2 us -> 86.3 us
    pallas_call x1, Pallas kernels: 87.3 us -> 84.4 us  [per_device(): pl.pallas_call(kernel, out_shape=shapes, in_specs=[anywhere] * 9, out_spe...]
where the time goes in v2:
time: 87.1 us; the launch traced here: 86.9 us
  Pallas kernels  86.3 us (99%)
    pallas_call x1, Pallas kernels, per_device(): pl.pallas_call(kernel, out_shape=shapes, in_specs=[anywhere] * 9, out_spe...  84.4 us
    pallas_call x1, Pallas kernels, per_device(): pl.pallas_call(hand_over, out_shape=shapes, in_specs=[vmem] * 5, out_spec...  1.85 us

profile of v2, /device:TPU:0, one launch (start us, length us, event | category | flops | bytes accessed | tf_op | source)
XLA Modules:
  0.0 86.9 jit_solution(7592823668319091692)
XLA Ops:
  0.6 84.4 %shard_map.128 = (bf16[128,1024]{1,0:T(8,128)(2,1)}, bf16[128,1024]{1,0:T(8,128)(2,1)}, f32[64,128]{1,0:T(8,128)}, f32[1,1024]{1,0:T(1,128)}, f32[1,1024]{1,0:T(1,128)}) custom-call(bf16[128,1024]{1,0:T(8,128)(2,1)} %qh_hbm.1, bf16[128,1024]{1,0:T(8,128)(2,1)} %dh_hbm.1, s32[1,128]{1,0:T(1,128)} %bitcast.14, s32[1,128]{1,0:T(1,128)} %bitcast.15, ...), custom_call_target="tpu_custom_call" | custom-call | flops 16000000000 | bytes 5000000 | tf_op jit(solution)/shard_map/pallas_call | solution.py:568
  85.1 1.9 %shard_map.129 = (bf16[128,1024]{1,0:T(8,128)(2,1)}, bf16[128,1024]{1,0:T(8,128)(2,1)}, f32[64,128]{1,0:T(8,128)}, f32[1,1024]{1,0:T(1,128)}, f32[1,1024]{1,0:T(1,128)}) custom-call(bf16[128,1024]{1,0:T(8,128)(2,1)} %get-tuple-element.15.refs_0_, bf16[128,1024]{1,0:T(8,128)(2,1)} %get-tuple-element.16.refs_1_, f32[64,128]{1,0:T(8,128)} %get-tuple-element.17.refs_2_, ...), custom_call_target="tpu_custom_call" | custom-call | bytes 1200000 | tf_op jit(solution)/shard_map/pallas_call | solution.py:582

commit v3 on v2

--- a/solution.py
+++ b/solution.py
@@ -341,8 +341,9 @@
 
     D = (gdp, dfold, dring, d_peer, quarter)
     Q = (sbuf, qfold, qring, q_peer, width // 4)
-    grads_of((2,), range(8))
+    grads(1 - core, 2, range(8))
     query_terms(2, 1)
+    grads(core, 2, range(8))
     query_terms(2, 0)
     grads_of((0, 1, 3), (4, 5))
     doc_terms(2)
@@ -390,22 +391,28 @@
         d_ring0 += merged(*D, 0, c, d_fold0)
         q_ring0 += merged(*Q, 0, c, q_fold0)
 
-    left = lax.broadcasted_iota(jnp.int32, (2 * rows, rows), 1) < half
+    left = lax.broadcasted_iota(jnp.int32, (rows, rows), 1) < half
+    ge_copies = []
+
+    def embed_rows(total, low):
+        span = slice(low, low + rows)
+        g_unit, uu = logit_scale * total, unit[span, :]
+        g = (g_unit - uu * jnp.sum(uu * g_unit, axis=1, keepdims=True)) * inv[span, :]
+        for j in range(4):
+            b0, b1 = g[:, 2 * j * rows : (2 * j + 1) * rows], g[:, (2 * j + 1) * rows : (2 * j + 2) * rows]
+            n0 = jnp.where(left, b0, pltpu.roll(b1, half, 1))
+            n1 = jnp.where(left, pltpu.roll(b0, half, 1), b1)
+            ge[span, j * rows : (j + 1) * rows] = jnp.where(core == 0, n0, n1).astype(bf16)
+            gs[span, j * rows : (j + 1) * rows] = jnp.where(core == 0, n1, n0).astype(bf16)
+        ge_copies.append(send(gs.at[pl.ds(low, rows), :], ge.at[pl.ds(2 * rows + low, rows), :], q_peer(0, 0, 1)))
+        return g.astype(bf16)
+
     arrive(*d_near0, *d_ring0, *d_across)
-    g_doc = ring_sum(gdp, dring, 0, 0, rows) + dx_buf[1].astype(f32)
+    g_doc = embed_rows(ring_sum(gdp, dring, 0, 0, rows) + dx_buf[1].astype(f32), rows)
     arrive(*q_near0, *q_ring0, *q_across)
-    g_query = (ring_sum(sbuf, qring, 0, 0, width) + qx[1].astype(f32)).T
-    g_unit = logit_scale * jnp.concatenate([g_query, g_doc], axis=0)
-    uu = unit[...]
-    g = (g_unit - uu * jnp.sum(uu * g_unit, axis=1, keepdims=True)) * inv[...]
-    for j in range(4):
-        b0, b1 = g[:, 2 * j * rows : (2 * j + 1) * rows], g[:, (2 * j + 1) * rows : (2 * j + 2) * rows]
-        n0 = jnp.where(left, b0, pltpu.roll(b1, half, 1))
-        n1 = jnp.where(left, pltpu.roll(b0, half, 1), b1)
-        ge[0 : 2 * rows, j * rows : (j + 1) * rows] = jnp.where(core == 0, n0, n1).astype(bf16)
-        gs[:, j * rows : (j + 1) * rows] = jnp.where(core == 0, n1, n0).astype(bf16)
-    ge_copy = send(gs, ge.at[pl.ds(2 * rows, 2 * rows), :], q_peer(0, 0, 1))
-    gn = lax.dot_general(g.astype(bf16), proj[...], NT, preferred_element_type=f32)
+    g_query = embed_rows((ring_sum(sbuf, qring, 0, 0, width) + qx[1].astype(f32)).T, 0)
+    g = jnp.concatenate([g_query, g_doc], axis=0)
+    gn = lax.dot_general(g, proj[...], NT, preferred_element_type=f32)
     nn = normed[...]
     gns[...] = gn
     gb[0:1, :] = jnp.sum(gn * nn, axis=0, keepdims=True)
@@ -415,7 +422,7 @@
     gba[order] = gb[...]
 
     low_left = left[:half]
-    arrive(out_sib, ge_copy)
+    arrive(out_sib, *ge_copies)
 
     def head(n, carry):
         for a in range(2):

time: 87.1 us -> 86.5 us (level)
  no operation moved by 1% of the time
where the time goes in v3:
time: 86.5 us; the launch traced here: 86.3 us
  Pallas kernels  85.7 us (99%)
    pallas_call x1, Pallas kernels, per_device(): pl.pallas_call(kernel, out_shape=shapes, in_specs=[anywhere] * 9, out_spe...  83.9 us
    pallas_call x1, Pallas kernels, per_device(): pl.pallas_call(hand_over, out_shape=shapes, in_specs=[vmem] * 5, out_spec...  1.85 us

profile of v3, /device:TPU:0, one launch (start us, length us, event | category | flops | bytes accessed | tf_op | source)
XLA Modules:
  0.0 86.3 jit_solution(9613139547301462333)
XLA Ops:
  0.6 83.9 %shard_map.128 = (bf16[128,1024]{1,0:T(8,128)(2,1)}, bf16[128,1024]{1,0:T(8,128)(2,1)}, f32[64,128]{1,0:T(8,128)}, f32[1,1024]{1,0:T(1,128)}, f32[1,1024]{1,0:T(1,128)}) custom-call(bf16[128,1024]{1,0:T(8,128)(2,1)} %qh_hbm.1, bf16[128,1024]{1,0:T(8,128)(2,1)} %dh_hbm.1, s32[1,128]{1,0:T(1,128)} %bitcast.14, s32[1,128]{1,0:T(1,128)} %bitcast.15, ...), custom_call_target="tpu_custom_call" | custom-call | flops 16000000000 | bytes 5000000 | tf_op jit(solution)/shard_map/pallas_call | solution.py:575
  84.5 1.9 %shard_map.129 = (bf16[128,1024]{1,0:T(8,128)(2,1)}, bf16[128,1024]{1,0:T(8,128)(2,1)}, f32[64,128]{1,0:T(8,128)}, f32[1,1024]{1,0:T(1,128)}, f32[1,1024]{1,0:T(1,128)}) custom-call(bf16[128,1024]{1,0:T(8,128)(2,1)} %get-tuple-element.15.refs_0_, bf16[128,1024]{1,0:T(8,128)(2,1)} %get-tuple-element.16.refs_1_, f32[64,128]{1,0:T(8,128)} %get-tuple-element.17.refs_2_, ...), custom_call_target="tpu_custom_call" | custom-call | bytes 1200000 | tf_op jit(solution)/shard_map/pallas_call | solution.py:589
